TPU v7x, 32 devices: a whole 2x2x4 slice. The times are simulated.
32 devices in a mesh: groups: 2 (over y), page: 4 (over z), tensor: 4 (over x, core).
Axes of the slice: x: 2, y: 2, z: 4, core: 2. Of those that a mesh axis runs over, the one named last changes fastest.
Arguments:
- query: bfloat16 [4096, 4096], P(('groups', 'page'), 'tensor'), parts along dimension 0, may hold values from -13 to 13
- memory: bfloat16 [2048, 1024], P(('groups', 'page'), 'tensor'), parts along dimension 0, may hold values from -20 to 20
- key_weight: bfloat16 [1024, 4096], P(None, 'tensor'), may hold values from -2.6 to 2.6
- value_weight: bfloat16 [1024, 4096], P(None, 'tensor'), may hold values from -0.1875 to 0.1875
- out_grad: bfloat16 [4096, 4096], P(('groups', 'page'), 'tensor'), parts along dimension 0, may hold values from -6 to 6
- mask_blocks: int32 [8, 3, 4, 2], P(('groups', 'page')), parts along dimension 0, may hold values from 0 to 1, as said below
Outputs:
- attended: bfloat16 [4096, 4096], P(('groups', 'page'), 'tensor'), parts along dimension 0
- query_grad: bfloat16 [4096, 4096], P(('groups', 'page'), 'tensor'), parts along dimension 0
- memory_grad: bfloat16 [2048, 1024], P(('groups', 'page'), 'tensor'), parts along dimension 0
There are 2 independent parts, one for each index of `groups`. A program takes and returns all parts, laid end to end along the dimension named above; an argument that names none is the same for every part. Nothing has to cross between parts.
Inputs may be any that keep to these rules, and one draw needn't show every extreme that they name: `mask_blocks`: for every page and every block of 128 query rows, at least one block of the page's own memory (slot 1) is marked.
All inputs are finite; a program needn't handle non-finite values.
Results may differ from a plain program's by a relative error of at most 0.02.
The roundings to bfloat16 on the way count: a program that leaves them out, or rounds other values in their place, can miss the bound.
Values may be sent and summed in bfloat16 or wider, within the bound.
A program may use at most 128 MiB of HBM per device.

v0:
```python
import math
import jax
import jax.numpy as jnp
from jax import lax
from jax.sharding import PartitionSpec as P

HD = 128
masked_score = -1e30


def padded(block, sides, width):
    for axis, dim in sides:
        count = lax.axis_size(axis)
        forward = [(i, i + 1) for i in range(count - 1)]
        backward = [(target, source) for source, target in forward]
        low = lax.ppermute(
            lax.slice_in_dim(block, block.shape[dim] - width, None, axis=dim), axis, forward
        )
        high = lax.ppermute(lax.slice_in_dim(block, 0, width, axis=dim), axis, backward)
        block = jnp.concatenate([low, block, high], axis=dim)
    return block


def from_behind(x, axis, by):
    devices = lax.axis_size(axis)
    pairs = [(i, i + by) for i in range(devices) if 0 <= i + by < devices]
    return lax.ppermute(x, axis, pairs)


def back_project(key_part, value_part, key_weight, value_weight):
    dims = (((1,), (1,)), ((), ()))
    return lax.dot_general(
        key_part, key_weight, dims, preferred_element_type=jnp.float32
    ) + lax.dot_general(value_part, value_weight, dims, preferred_element_type=jnp.float32)


def on_device(query, memory, key_weight, value_weight, out_grad, mask_blocks):
    token_rows = query.shape[0]
    features = query.shape[1]
    head_count = features // HD
    memory_rows = memory.shape[0]
    page_index = lax.axis_index("page")
    page_total = lax.axis_size("page")
    memory_rim = padded(memory, (("page", 0),), memory_rows)
    wide_memory = lax.all_gather(memory_rim, "tensor", axis=1, tiled=True)
    key_slab = jnp.dot(wide_memory, key_weight, preferred_element_type=jnp.float32).astype(
        jnp.bfloat16
    )
    value_slab = jnp.dot(wide_memory, value_weight, preferred_element_type=jnp.float32).astype(
        jnp.bfloat16
    )
    sources = page_index + jnp.arange(3, dtype=jnp.int32) - 1
    source_live = ((sources >= 0) & (sources < page_total)).astype(jnp.float32)
    block_grid = mask_blocks[0].astype(jnp.float32) * source_live[:, None, None]
    query_blocks = block_grid.shape[1]
    memory_blocks = block_grid.shape[2]
    block_size = token_rows // query_blocks
    spread_grid = jnp.transpose(block_grid, (1, 0, 2))[:, None, :, :, None]
    visible = jnp.broadcast_to(
        spread_grid, (query_blocks, block_size, 3, memory_blocks, block_size)
    ).reshape(token_rows, 3 * memory_rows)
    score_scale = 1.0 / math.sqrt(HD)
    query_heads = query.reshape(token_rows, head_count, HD)
    key_heads = key_slab.reshape(3 * memory_rows, head_count, HD)
    value_heads = value_slab.reshape(3 * memory_rows, head_count, HD)
    scores = (
        jnp.einsum("thd,khd->htk", query_heads, key_heads, preferred_element_type=jnp.float32)
        * score_scale
    )
    scores = jnp.where(visible[None] > 0, scores, masked_score)
    row_max = jnp.max(scores, axis=2, keepdims=True)
    exponent = jnp.exp(scores - row_max)
    weights = exponent / jnp.sum(exponent, axis=2, keepdims=True)
    rounded_weights = weights.astype(jnp.bfloat16)
    mixed = jnp.einsum(
        "htk,khd->thd", rounded_weights, value_heads, preferred_element_type=jnp.float32
    )
    attended = mixed.reshape(token_rows, features).astype(jnp.bfloat16)
    grad_rows = out_grad.reshape(token_rows, head_count, HD)
    weight_grad = jnp.einsum(
        "thd,khd->htk", grad_rows, value_heads, preferred_element_type=jnp.float32
    )
    row_inner = jnp.sum(weights * weight_grad, axis=2, keepdims=True)
    score_grad = (weights * (weight_grad - row_inner) * score_scale).astype(jnp.bfloat16)
    query_grad = jnp.einsum(
        "htk,khd->thd", score_grad, key_heads, preferred_element_type=jnp.float32
    )
    query_grad = query_grad.reshape(token_rows, features).astype(jnp.bfloat16)
    key_piece = jnp.einsum(
        "htk,thd->khd", score_grad, query_heads, preferred_element_type=jnp.float32
    )
    key_piece = key_piece.reshape(3 * memory_rows, features).astype(jnp.bfloat16)
    value_piece = jnp.einsum(
        "htk,thd->khd", rounded_weights, grad_rows, preferred_element_type=jnp.float32
    )
    value_piece = value_piece.reshape(3 * memory_rows, features).astype(jnp.bfloat16)
    toward_previous = jnp.stack([key_piece[:memory_rows], value_piece[:memory_rows]])
    toward_next = jnp.stack([key_piece[2 * memory_rows :], value_piece[2 * memory_rows :]])
    from_next = from_behind(toward_previous, "page", -1)
    from_prev = from_behind(toward_next, "page", 1)
    partial_value = back_project(
        key_piece[memory_rows : 2 * memory_rows],
        value_piece[memory_rows : 2 * memory_rows],
        key_weight,
        value_weight,
    )
    partial_value = partial_value + back_project(
        from_next[0], from_next[1], key_weight, value_weight
    )
    partial_value = partial_value + back_project(
        from_prev[0], from_prev[1], key_weight, value_weight
    )
    summed = lax.psum_scatter(
        partial_value.astype(jnp.bfloat16), "tensor", scatter_dimension=1, tiled=True
    )
    return (attended, query_grad, summed)


def solution(mesh):
    placed = (
        P(("groups", "page"), "tensor"),
        P(("groups", "page"), "tensor"),
        P(None, "tensor"),
        P(None, "tensor"),
        P(("groups", "page"), "tensor"),
        P(("groups", "page"), None, None, None),
    )
    return jax.shard_map(
        on_device,
        mesh=mesh,
        in_specs=placed,
        out_specs=(
            P(("groups", "page"), "tensor"),
            P(("groups", "page"), "tensor"),
            P(("groups", "page"), "tensor"),
        ),
        check_vma=False,
    )
```

profile of v0, /device:TPU:0, one launch (start us, length us, event | category | flops | bytes accessed | tf_op | source)
XLA Modules:
  0.0 164.3 jit_solution(5907997166472424290)
XLA Ops:
  7.2 0.0 copy-start
  7.2 0.0 all-gather.2.cloned.1.call-start
  7.2 1.4 collective-permute-start.1
  8.7 5.6 %collective-permute-start = (bf16[256,256]{1,0:T(8,128)(2,1)}, bf16[256,256]{1,0:T(8,128)(2,1)S(1)}, u32[]{:S(2)}, u32[]{:S(2)}) collective-permute-start(bf16[256,256]{1,0:T(8,128)(2,1)} %param.7), channel_id=1, source_target_pairs={{0,4},{4,8},{8,12},{1,5},{5,9},{9,13},{2,6},{6,10},{10,14},{3,7},{... | collective-permute-start | bytes 393224 | tf_op jit(solution)/shard_map/ppermute | solution.py:16
  14.2 1.8 %collective-permute-done.1 = bf16[256,256]{1,0:T(8,128)(2,1)S(1)} collective-permute-done((bf16[256,256]{1,0:T(8,128)(2,1)}, bf16[256,256]{1,0:T(8,128)(2,1)S(1)}, u32[]{:S(2)}, u32[]{:S(2)}) %collective-permute-start.1) | collective-permute-done | bytes 131104 | tf_op jit(solution)/shard_map/ppermute | solution.py:19
  16.0 1.3 collective-permute-done
  17.3 1.7 %pad_maximum_fusion.2 = bf16[768,256]{1,0:T(8,128)(2,1)} fusion(bf16[256,256]{1,0:T(8,128)(2,1)S(1)} %collective-permute-done.1, bf16[256,256]{1,0:T(8,128)(2,1)} %param.7, bf16[256,256]{1,0:T(8,128)(2,1)S(1)} %collective-permute-done), kind=kLoop, calls=%fused_computation.51 | loop fusion | flops 1179648 | bytes 786432 | tf_op jit(solution)/shard_map/concatenate | solution.py:20
  18.9 0.0 all-gather.2.cloned.1.call-update
  19.0 0.0 reduce-scatter.2.cloned.1.call-start
  19.0 0.8 compare_bitcast_fusion
  19.8 0.3 broadcast_in_dim.14
  20.1 0.2 copy.41
  20.3 2.3 %copy.28 = bf16[512,1024]{0,1:T(8,128)(2,1)} copy(bf16[512,1024]{1,0:T(8,128)(2,1)} %param.6) | data formatting | bytes 2097152 | tf_op jit(solution)/shard_map/reshape | solution.py:63
  22.6 1.5 copy.29
  24.1 17.2 %all-gather.2.cloned.1.call-done = bf16[768,1024]{1,0:T(8,128)(2,1)} async-done(((bf16[768,256]{1,0:T(8,128)(2,1)}), bf16[768,1024]{1,0:T(8,128)(2,1)}) %all-gather.2.cloned.1.call-update) | async-done | bytes 1572880 | tf_op jit(solution)/shard_map/all_gather | solution.py:45
  41.2 5.0 %convolution_convert_fusion = bf16[768,1024]{1,0:T(8,128)(2,1)} fusion(bf16[768,1024]{1,0:T(8,128)(2,1)} %all-gather.2.cloned.1.call-done, bf16[1024,1024]{1,0:T(8,128)(2,1)} %param.8), kind=kOutput, calls=%fused_computation.23 | convolution fusion | flops 1611399168 | bytes 5242880 | tf_op jit(solution)/shard_map/dot_general | solution.py:46
  46.3 2.6 %copy.27 = bf16[768,1024]{0,1:T(8,128)(2,1)} copy(bf16[768,1024]{1,0:T(8,128)(2,1)} %convolution_convert_fusion) | data formatting | bytes 3145728 | tf_op jit(solution)/shard_map/reshape | solution.py:64
  48.9 0.0 copy-done
  48.9 3.2 %fusion.26 = bf16[96,8,8,128]{3,2,1,0:T(8,128)(2,1)S(1)} fusion(bf16[768,1024]{1,0:T(8,128)(2,1)} %all-gather.2.cloned.1.call-done, bf16[1024,1024]{1,0:T(8,128)(2,1)S(1)} %copy-done), kind=kOutput, calls=%fused_computation.30 | convolution fusion | flops 1611399168 | bytes 5242880 | tf_op jit(solution)/shard_map/dot_general | solution.py:49
  52.1 0.0 copy-start.2
  52.1 6.3 %fusion.21 = f32[8,768,512]{2,1,0:T(8,128)} fusion(bf16[512,8,128]{0,2,1:T(8,128)(2,1)S(1)} %bitcast.118, bf16[96,8,8,128]{3,2,1,0:T(8,128)(2,1)S(1)} %fusion.26), kind=kOutput, calls=%fused_computation.26 | convolution fusion | flops 805306368 | bytes 15204352 | tf_op jit(solution)/shard_map/thd,khd->htk/dot_general | solution.py:80
  58.4 0.0 copy-done.2
  58.4 11.0 %fusion.51 = (f32[8,512]{1,0:T(8,128)S(1)}, f32[8,512,768]{1,2,0:T(8,128)}) fusion(pred[512,768]{0,1:T(8,128)(4,1)S(1)} %bitcast.133, bf16[768,8,128]{0,2,1:T(8,128)(2,1)} %bitcast.126, bf16[512,8,128]{0,2,1:T(8,128)(2,1)} %bitcast.129), kind=kOutput, calls=%fused_computation.63 | convolution fusion | flops 817890048 | bytes 15613952 | tf_op jit(solution)/shard_map/sub | solution.py:72
  69.4 8.0 %fusion.23 = bf16[768,8,128]{0,2,1:T(8,128)(2,1)} fusion(bf16[512,8,128]{0,2,1:T(8,128)(2,1)S(1)} %bitcast.119, f32[8,512,768]{1,2,0:T(8,128)} %get-tuple-element.13, f32[8,512]{1,0:T(8,128)S(1)} %get-tuple-element.12), kind=kOutput, calls=%fused_computation.29 | convolution fusion | flops 812384256 | bytes 15220736 | tf_op jit(solution)/shard_map/htk,thd->khd/dot_general | solution.py:93
  77.4 18.9 %fusion.27 = bf16[768,8,128]{0,2,1:T(8,128)(2,1)} fusion(bf16[512,8,128]{0,2,1:T(8,128)(2,1)} %bitcast.130, f32[8,768,512]{2,1,0:T(8,128)} %fusion.21, f32[8,512,768]{1,2,0:T(8,128)} %get-tuple-element.13, f32[8,512]{1,0:T(8,128)S(1)} %get-tuple-element.12), kind=kOutput, calls=%fused_computation.31 | convolution fusion | flops 828117760 | bytes 27803648 | tf_op jit(solution)/shard_map/htk,thd->khd/dot_general | solution.py:89
  96.3 0.0 copy-start.3
  96.3 1.6 fusion.49
  97.9 0.3 copy-done.3
  98.2 0.0 copy-start.1
  98.2 0.2 fusion.50
  98.4 0.1 pad_maximum_fusion
  98.5 1.4 collective-permute-start.2
  99.9 0.1 pad_maximum_fusion.1
  100.0 4.6 %collective-permute-start.3 = (bf16[2,256,1024]{1,2,0:T(8,128)(2,1)S(1)}, bf16[2,256,1024]{1,2,0:T(8,128)(2,1)S(1)}, u32[]{:S(2)}, u32[]{:S(2)}) collective-permute-start(bf16[2,256,1024]{1,2,0:T(8,128)(2,1)S(1)} %pad_maximum_fusion.1), channel_id=1, source_target_pairs={{0,4},{4,8},{8,12},{1,5},{5,9},{9,13},{2,6},{6,10},{10,14},{3,7},{... | collective-permute-start | bytes 3145736 | tf_op jit(solution)/shard_map/ppermute | solution.py:27
  104.6 0.0 copy-done.1
  104.6 0.8 fusion.52
  105.4 0.8 convolution_add_fusion.2
  106.2 19.6 %collective-permute-done.2 = bf16[2,256,1024]{1,2,0:T(8,128)(2,1)S(1)} collective-permute-done((bf16[2,256,1024]{1,2,0:T(8,128)(2,1)S(1)}, bf16[2,256,1024]{1,2,0:T(8,128)(2,1)S(1)}, u32[]{:S(2)}, u32[]{:S(2)}) %collective-permute-start.2) | collective-permute-done | bytes 1048608 | tf_op jit(solution)/shard_map/ppermute | solution.py:27
  125.8 0.8 fusion.42
  126.6 0.5 collective-permute-done.3
  127.1 0.8 fusion.41
  127.9 0.8 fusion.37
  128.7 1.6 fusion.38
  130.2 0.0 reduce-scatter.2.cloned.1.call-update
  130.3 6.3 %fusion.28 = bf16[8,128,512]{2,1,0:T(8,128)(2,1)S(1)} fusion(bf16[96,8,8,128]{3,2,1,0:T(8,128)(2,1)} %copy-done.2, f32[8,512,768]{1,2,0:T(8,128)} %get-tuple-element.13, f32[8,512]{1,0:T(8,128)S(1)} %get-tuple-element.12), kind=kOutput, calls=%fused_computation.32 | convolution fusion | flops 812122112 | bytes 15220736 | tf_op jit(solution)/shard_map/htk,khd->thd/dot_general | solution.py:75
  136.6 1.3 copy.21
  137.9 18.3 %fusion.33 = bf16[8,128,512]{2,1,0:T(8,128)(2,1)S(1)} fusion(bf16[768,8,128]{0,2,1:T(8,128)(2,1)} %bitcast.127, f32[8,768,512]{2,1,0:T(8,128)} %fusion.21, f32[8,512,768]{1,2,0:T(8,128)} %get-tuple-element.13, f32[8,512]{1,0:T(8,128)S(1)} %get-tuple-element.12), kind=kOutput, calls=%fused_computation.33 | convolution fusion | flops 827855616 | bytes 27803648 | tf_op jit(solution)/shard_map/htk,khd->thd/dot_general | solution.py:85
  156.1 1.3 copy.22
  157.5 0.0 reduce-scatter.2.cloned.1.call-done
  (1 shorter events, 0.0 us)
Async XLA Ops:
  7.2 41.8 %copy-start = (bf16[1024,1024]{1,0:T(8,128)(2,1)S(1)}, bf16[1024,1024]{1,0:T(8,128)(2,1)}, u32[]{:S(2)}) copy-start(bf16[1024,1024]{1,0:T(8,128)(2,1)} %param.9) | copy-start | bytes 6291460
  7.2 34.1 %all-gather.2.cloned.1.call-start = ((), (), s32[]{:S(2)}) async-start(), calls=%async_computation.1 | async-start | bytes 1966080 | tf_op jit(solution)/shard_map/all_gather | solution.py:45
  7.2 8.8 %collective-permute-start.1 = (bf16[256,256]{1,0:T(8,128)(2,1)}, bf16[256,256]{1,0:T(8,128)(2,1)S(1)}, u32[]{:S(2)}, u32[]{:S(2)}) collective-permute-start(bf16[256,256]{1,0:T(8,128)(2,1)} %param.7), channel_id=1, source_target_pairs={{4,0},{8,4},{12,8},{5,1},{9,5},{13,9},{6,2},{10,6},{14,10},{7,3},{... | collective-permute-start | bytes 393224 | tf_op jit(solution)/shard_map/ppermute | solution.py:19
  8.7 8.6 %collective-permute-start = (bf16[256,256]{1,0:T(8,128)(2,1)}, bf16[256,256]{1,0:T(8,128)(2,1)S(1)}, u32[]{:S(2)}, u32[]{:S(2)}) collective-permute-start(bf16[256,256]{1,0:T(8,128)(2,1)} %param.7), channel_id=1, source_target_pairs={{0,4},{4,8},{8,12},{1,5},{5,9},{9,13},{2,6},{6,10},{10,14},{3,7},{... | collective-permute-start | bytes 393224 | tf_op jit(solution)/shard_map/ppermute | solution.py:16
  19.0 138.5 %reduce-scatter.2.cloned.1.call-start = ((), (), s32[]{:S(2)}) async-start(), calls=%async_computation.2 | async-start | bytes 655360 | tf_op jit(solution)/shard_map/reduce_scatter | solution.py:113
  52.1 6.3 %copy-start.2 = (bf16[96,8,8,128]{3,2,1,0:T(8,128)(2,1)}, bf16[96,8,8,128]{3,2,1,0:T(8,128)(2,1)S(1)}, u32[]{:S(2)}) copy-start(bf16[96,8,8,128]{3,2,1,0:T(8,128)(2,1)S(1)} %fusion.26) | copy-start | bytes 4718596
  96.3 1.9 %copy-start.3 = (bf16[768,8,128]{0,2,1:T(8,128)(2,1)S(1)}, bf16[768,8,128]{0,2,1:T(8,128)(2,1)}, u32[]{:S(2)}) copy-start(bf16[768,8,128]{0,2,1:T(8,128)(2,1)} %fusion.23) | copy-start | bytes 4718596
  98.2 6.4 %copy-start.1 = (bf16[1024,1024]{1,0:T(8,128)(2,1)S(1)}, bf16[1024,1024]{1,0:T(8,128)(2,1)}, u32[]{:S(2)}) copy-start(bf16[1024,1024]{1,0:T(8,128)(2,1)} %param.8) | copy-start | bytes 6291460
  98.5 27.3 %collective-permute-start.2 = (bf16[2,256,1024]{1,2,0:T(8,128)(2,1)S(1)}, bf16[2,256,1024]{1,2,0:T(8,128)(2,1)S(1)}, u32[]{:S(2)}, u32[]{:S(2)}) collective-permute-start(bf16[2,256,1024]{1,2,0:T(8,128)(2,1)S(1)} %pad_maximum_fusion), channel_id=1, source_target_pairs={{4,0},{8,4},{12,8},{5,1},{9,5},{13,9},{6,2},{10,6},{14,10},{7,3},{... | collective-permute-start | bytes 3145736 | tf_op jit(solution)/shard_map/ppermute | solution.py:27
  100.0 27.1 %collective-permute-start.3 = (bf16[2,256,1024]{1,2,0:T(8,128)(2,1)S(1)}, bf16[2,256,1024]{1,2,0:T(8,128)(2,1)S(1)}, u32[]{:S(2)}, u32[]{:S(2)}) collective-permute-start(bf16[2,256,1024]{1,2,0:T(8,128)(2,1)S(1)} %pad_maximum_fusion.1), channel_id=1, source_target_pairs={{0,4},{4,8},{8,12},{1,5},{5,9},{9,13},{2,6},{6,10},{10,14},{3,7},{... | collective-permute-start | bytes 3145736 | tf_op jit(solution)/shard_map/ppermute | solution.py:27
Sparse Core Ops, SparseCore 0:
  19.1 22.1 all-gather.1
  130.4 22.8 reduce-scatter.1
where the time goes:
time: 165 us; the launch traced here: 164 us
  matrix products  82.4 us (50%)
  waiting for transfers between devices  40.4 us (24%)
  between operations  14.2 us (9%)
  starting transfers between devices  13.1 us (8%)
  local copies, waits for them, and re-layouts  11.6 us (7%)
  other arithmetic  2.64 us (2%)
    ppermute x2, waiting for transfers between devices, from_behind(): return lax.ppermute(x, axis, pairs)  20.1 us
    dot_general x1, matrix products, on_device(): jnp.einsum('htk,thd->khd', score_grad, query_heads, preferred_element_typ...  18.9 us
    dot_general x1, matrix products, on_device(): jnp.einsum('htk,khd->thd', score_grad, key_heads, preferred_element_type=...  18.3 us
    all_gather x1, waiting for transfers between devices, on_device(): wide_memory = lax.all_gather(memory_rim, 'tensor', axis=1, tiled=True)  17.2 us
    sub x1, matrix products, on_device(): exponent = jnp.exp(scores - row_max)  11 us
    dot_general x1, matrix products, on_device(): jnp.einsum('htk,thd->khd', rounded_weights, grad_rows, preferred_element_...  7.97 us
    dot_general x1, matrix products, on_device(): jnp.einsum('htk,khd->thd', rounded_weights, value_heads, preferred_elemen...  6.29 us
    dot_general x1, matrix products, on_device(): jnp.einsum('thd,khd->htk', grad_rows, value_heads, preferred_element_type...  6.26 us
  transfers between devices with their start and end apart: 6, of which 5 were waited for; matrix products, arithmetic and copies ran while one was open for 21% of the time, Pallas kernels for 0%

commit v1 on v0

--- a/solution.py
+++ b/solution.py
@@ -6,6 +6,12 @@
 
 HD = 128
 masked_score = -1e30
+
+
+def in_order(tiles, dim):
+    dims = list(tiles.shape[1:])
+    dims[dim] *= tiles.shape[0]
+    return jnp.moveaxis(tiles, 0, dim).reshape(dims)
 
 
 def padded(block, sides, width):
@@ -42,7 +48,19 @@
     page_index = lax.axis_index("page")
     page_total = lax.axis_size("page")
     memory_rim = padded(memory, (("page", 0),), memory_rows)
-    wide_memory = lax.all_gather(memory_rim, "tensor", axis=1, tiled=True)
+    devices_2 = lax.axis_size("tensor")
+    pairs_2 = [(i_2, (i_2 + 1) % devices_2) for i_2 in range(devices_2)]
+    back = [(b, a) for a, b in pairs_2]
+    lower, upper = ([], [])
+    for lap in range(devices_2 - 1):
+        if lap % 2 == 0:
+            lower.append(lax.ppermute(lower[-1] if lower else memory_rim, "tensor", pairs_2))
+        else:
+            upper.append(lax.ppermute(upper[-1] if upper else memory_rim, "tensor", back))
+    tiles = jnp.stack([*lower[::-1], memory_rim, *upper])
+    shift = lax.axis_index("tensor") - len(lower)
+    tiles = tiles[(jnp.arange(devices_2) - shift) % devices_2]
+    wide_memory = in_order(tiles, 1)
     key_slab = jnp.dot(wide_memory, key_weight, preferred_element_type=jnp.float32).astype(
         jnp.bfloat16
     )

time: 165 us -> 169 us (1.024)
  local copies, waits for them, and re-layouts: 11.6 us -> 18.1 us
  waiting for transfers between devices: 40.4 us -> 35.2 us
    all_gather x1 -> x0, waiting for transfers between devices: 17.2 us -> none  [on_device(): wide_memory = lax.all_gather(memory_rim, 'tensor', axis=1, tiled=True)]
    ppermute x0 -> x3, waiting for transfers between devices: none -> 10.5 us  [the longest x2 10.5 us: on_device(): lax.ppermute(lower[-1] if lower else memory_rim, 'tensor', pairs_2)]
    gather x0 -> x1, local copies, waits for them, and re-layouts: none -> 3.2 us  [on_device(): tiles = tiles[(jnp.arange(devices_2) - shift) % devices_2]]
    transpose x0 -> x1, local copies, waits for them, and re-layouts: none -> 2.59 us  [in_order(): return jnp.moveaxis(tiles, 0, dim).reshape(dims)]
    another operation x0 -> x1, other arithmetic: none -> 2.59 us  [on_device(): tiles = jnp.stack([*lower[::-1], memory_rim, *upper])]
    dot_general x1, matrix products: 5.02 us -> 3 us  [on_device(): jnp.dot(wide_memory, key_weight, preferred_element_type=jnp.float32)]
    ppermute x0 -> x3, starting transfers between devices: none -> 1.85 us  [the longest x1 1.72 us: on_device(): lax.ppermute(upper[-1] if upper else memory_rim, 'tensor', back)]
    unnamed x11 -> x19, local copies, waits for them, and re-layouts: 3.13 us -> 4.82 us
  transfers between devices with their start and end apart: 6 -> 8, of which waited for: 5 -> 6; matrix products, arithmetic and copies ran while one was open for 21% -> 21% of each run, Pallas kernels for 0% -> 0%
where the time goes in v1:
time: 169 us
  matrix products  83.2 us (49%)
  waiting for transfers between devices  35.2 us (21%)
  local copies, waits for them, and re-layouts  18.1 us (11%)
  starting transfers between devices  14.6 us (9%)
  between operations  14.3 us (8%)
  other arithmetic  3.57 us (2%)
    ppermute x2, waiting for transfers between devices, from_behind(): return lax.ppermute(x, axis, pairs)  19.8 us
    dot_general x1, matrix products, on_device(): jnp.einsum('htk,thd->khd', score_grad, query_heads, preferred_element_typ...  18.9 us
    dot_general x1, matrix products, on_device(): jnp.einsum('htk,khd->thd', score_grad, key_heads, preferred_element_type=...  18.3 us
    sub x1, matrix products, on_device(): exponent = jnp.exp(scores - row_max)  11 us
    ppermute x2, waiting for transfers between devices, on_device(): lax.ppermute(lower[-1] if lower else memory_rim, 'tensor', pairs_2)  10.5 us
    dot_general x1, matrix products, on_device(): jnp.einsum('htk,thd->khd', rounded_weights, grad_rows, preferred_element_...  7.97 us
    dot_general x1, matrix products, on_device(): jnp.einsum('thd,khd->htk', grad_rows, value_heads, preferred_element_type...  7.72 us
    dot_general x1, matrix products, on_device(): jnp.einsum('htk,khd->thd', rounded_weights, value_heads, preferred_elemen...  6.29 us
  transfers between devices with their start and end apart: 8, of which 6 were waited for; matrix products, arithmetic and copies ran while one was open for 21% of the time, Pallas kernels for 0%

profile of v1, /device:TPU:0, one launch (start us, length us, event | category | flops | bytes accessed | tf_op | source)
XLA Modules:
  0.0 168.9 jit_solution(17556644474784105043)
XLA Ops:
  7.2 0.0 copy-start
  7.2 0.0 copy-start.5
  7.2 0.0 reduce-scatter.2.cloned.1.call-start
  7.2 5.2 %collective-permute-start = (bf16[256,256]{1,0:T(8,128)(2,1)}, bf16[256,256]{1,0:T(8,128)(2,1)S(1)}, u32[]{:S(2)}, u32[]{:S(2)}) collective-permute-start(bf16[256,256]{1,0:T(8,128)(2,1)} %param.7), channel_id=1, source_target_pairs={{0,4},{4,8},{8,12},{1,5},{5,9},{9,13},{2,6},{6,10},{10,14},{3,7},{... | collective-permute-start | bytes 393224 | tf_op jit(solution)/shard_map/ppermute | solution.py:22
  12.4 1.3 collective-permute-start.1
  13.7 1.7 %collective-permute-done = bf16[256,256]{1,0:T(8,128)(2,1)S(1)} collective-permute-done((bf16[256,256]{1,0:T(8,128)(2,1)}, bf16[256,256]{1,0:T(8,128)(2,1)S(1)}, u32[]{:S(2)}, u32[]{:S(2)}) %collective-permute-start) | collective-permute-done | bytes 131104 | tf_op jit(solution)/shard_map/ppermute | solution.py:22
  15.5 0.9 constant_dynamic-update-slice_fusion.1
  16.4 3.1 %collective-permute-done.1 = bf16[256,256]{1,0:T(8,128)(2,1)S(1)} collective-permute-done((bf16[256,256]{1,0:T(8,128)(2,1)}, bf16[256,256]{1,0:T(8,128)(2,1)S(1)}, u32[]{:S(2)}, u32[]{:S(2)}) %collective-permute-start.1) | collective-permute-done | bytes 131104 | tf_op jit(solution)/shard_map/ppermute | solution.py:25
  19.5 0.1 collective-permute-start.2
  19.6 1.7 %collective-permute-start.4 = (bf16[768,256]{1,0:T(8,128)(2,1)S(1)}, bf16[768,256]{1,0:T(8,128)(2,1)}, u32[]{:S(2)}, u32[]{:S(2)}) collective-permute-start(bf16[768,256]{1,0:T(8,128)(2,1)S(1)} %constant_dynamic-update-slice_fusion), channel_id=1, source_target_pairs={{1,0},{2,1},{3,2},{0,3},{5,4},{6,5},{7,6},{4,7},{9,8},{10,9},{11,1... | collective-permute-start | bytes 1179656 | tf_op jit(solution)/shard_map/ppermute | solution.py:59
  21.3 7.9 %collective-permute-done.2 = bf16[768,256]{1,0:T(8,128)(2,1)} collective-permute-done((bf16[768,256]{1,0:T(8,128)(2,1)S(1)}, bf16[768,256]{1,0:T(8,128)(2,1)}, u32[]{:S(2)}, u32[]{:S(2)}) %collective-permute-start.2) | collective-permute-done | bytes 393248 | tf_op jit(solution)/shard_map/ppermute | solution.py:57
  29.2 0.1 collective-permute-start.3
  29.3 0.8 compare_bitcast_fusion
  30.1 0.3 broadcast_in_dim.14
  30.4 0.9 copy.70
  31.3 0.0 copy-done.5
  31.3 1.3 copy.57
  32.6 1.5 copy.58
  34.1 0.0 collective-permute-done.4
  34.2 2.6 %collective-permute-done.3 = bf16[768,256]{1,0:T(8,128)(2,1)} collective-permute-done((bf16[768,256]{1,0:T(8,128)(2,1)}, bf16[768,256]{1,0:T(8,128)(2,1)}, u32[]{:S(2)}, u32[]{:S(2)}) %collective-permute-start.3) | collective-permute-done | bytes 393248 | tf_op jit(solution)/shard_map/ppermute | solution.py:57
  36.8 2.6 %pad_maximum_fusion = bf16[4,768,256]{2,1,0:T(8,128)(2,1)} fusion(bf16[1,768,256]{2,1,0:T(8,128)(2,1)} %bitcast.3, bf16[1,768,256]{2,1,0:T(8,128)(2,1)S(1)} %bitcast.144, bf16[1,768,256]{2,1,0:T(8,128)(2,1)} %bitcast.1, bf16[1,768,256]{2,1,0:T(8,128)(2,1)} %bitcast), kind=kLoop, calls=%fused_computation.29 | loop fusion | flops 2359296 | bytes 3145728 | tf_op jit(solution)/shard_map/stack | solution.py:60
  39.3 3.2 %gather_fusion = bf16[4,768,256]{2,1,0:T(8,128)(2,1)} fusion(bf16[4,768,256]{2,1,0:T(8,128)(2,1)} %pad_maximum_fusion, s32[1024]{0:T(1024)S(1)} %pad_clamp_fusion), kind=kCustom, calls=%fused_computation | custom fusion | bytes 3145744 | tf_op jit(solution)/shard_map/gather | solution.py:62
  42.5 2.6 %copy.37 = bf16[768,4,256]{0,2,1:T(8,128)(2,1)} copy(bf16[768,4,256]{2,0,1:T(8,128)(2,1)} %bitcast.126) | data formatting | bytes 3145728 | tf_op jit(solution)/shard_map/transpose | solution.py:14
  45.1 0.0 copy-done
  45.1 0.0 copy-start.1
  45.1 0.0 copy-start.4
  45.1 4.6 %fusion.26 = bf16[96,8,8,128]{3,2,1,0:T(8,128)(2,1)} fusion(bf16[768,1024]{0,1:T(8,128)(2,1)} %bitcast.137, bf16[1024,1024]{1,0:T(8,128)(2,1)S(1)} %copy-done), kind=kOutput, calls=%fused_computation.32 | convolution fusion | flops 1611399168 | bytes 5242880 | tf_op jit(solution)/shard_map/dot_general | solution.py:67
  49.8 0.0 copy-done.1
  49.8 0.0 copy-done.4
  49.8 3.0 %convolution_convert_fusion = bf16[768,1024]{1,0:T(8,128)(2,1)} fusion(bf16[768,1024]{0,1:T(8,128)(2,1)S(1)} %bitcast.138, bf16[1024,1024]{1,0:T(8,128)(2,1)S(1)} %copy-done.1), kind=kOutput, calls=%fused_computation.24 | convolution fusion | flops 1611399168 | bytes 5242880 | tf_op jit(solution)/shard_map/dot_general | solution.py:64
  52.8 2.6 %copy.56 = bf16[768,1024]{0,1:T(8,128)(2,1)} copy(bf16[768,1024]{1,0:T(8,128)(2,1)} %convolution_convert_fusion) | data formatting | bytes 3145728 | tf_op jit(solution)/shard_map/reshape | solution.py:82
  55.3 0.0 copy-start.6
  55.3 7.7 %fusion.21 = f32[8,768,512]{2,1,0:T(8,128)} fusion(bf16[512,8,128]{0,2,1:T(8,128)(2,1)S(1)} %bitcast.127, bf16[96,8,8,128]{3,2,1,0:T(8,128)(2,1)} %fusion.26), kind=kOutput, calls=%fused_computation.27 | convolution fusion | flops 805306368 | bytes 15204352 | tf_op jit(solution)/shard_map/thd,khd->htk/dot_general | solution.py:98
  63.1 0.0 copy-done.6
  63.1 11.0 %fusion.53 = (f32[8,512]{1,0:T(8,128)S(1)}, f32[8,512,768]{1,2,0:T(8,128)}) fusion(pred[512,768]{0,1:T(8,128)(4,1)S(1)} %bitcast.145, bf16[768,8,128]{0,2,1:T(8,128)(2,1)} %bitcast.135, bf16[512,8,128]{0,2,1:T(8,128)(2,1)} %bitcast.140), kind=kOutput, calls=%fused_computation.74 | convolution fusion | flops 817890048 | bytes 15613952 | tf_op jit(solution)/shard_map/sub | solution.py:90
  74.1 8.0 %fusion.23 = bf16[768,8,128]{0,2,1:T(8,128)(2,1)} fusion(bf16[512,8,128]{0,2,1:T(8,128)(2,1)S(1)} %bitcast.128, f32[8,512,768]{1,2,0:T(8,128)} %get-tuple-element.19, f32[8,512]{1,0:T(8,128)S(1)} %get-tuple-element.18), kind=kOutput, calls=%fused_computation.31 | convolution fusion | flops 812384256 | bytes 15220736 | tf_op jit(solution)/shard_map/htk,thd->khd/dot_general | solution.py:111
  82.1 18.9 %fusion.27 = bf16[768,8,128]{0,2,1:T(8,128)(2,1)} fusion(bf16[512,8,128]{0,2,1:T(8,128)(2,1)} %bitcast.141, f32[8,768,512]{2,1,0:T(8,128)} %fusion.21, f32[8,512,768]{1,2,0:T(8,128)} %get-tuple-element.19, f32[8,512]{1,0:T(8,128)S(1)} %get-tuple-element.18), kind=kOutput, calls=%fused_computation.33 | convolution fusion | flops 828117760 | bytes 27803648 | tf_op jit(solution)/shard_map/htk,thd->khd/dot_general | solution.py:107
  100.9 0.0 copy-start.3
  100.9 1.6 fusion.51
  102.6 0.3 copy-done.3
  102.8 0.2 fusion.52
  103.0 0.0 copy-start.2
  103.0 0.1 pad_maximum_fusion.1
  103.1 1.4 collective-permute-start.5
  104.6 0.1 pad_maximum_fusion.2
  104.7 4.8 %collective-permute-start.6 = (bf16[2,256,1024]{1,2,0:T(8,128)(2,1)S(1)}, bf16[2,256,1024]{1,2,0:T(8,128)(2,1)S(1)}, u32[]{:S(2)}, u32[]{:S(2)}) collective-permute-start(bf16[2,256,1024]{1,2,0:T(8,128)(2,1)S(1)} %pad_maximum_fusion.2), channel_id=1, source_target_pairs={{0,4},{4,8},{8,12},{1,5},{5,9},{9,13},{2,6},{6,10},{10,14},{3,7},{... | collective-permute-start | bytes 3145736 | tf_op jit(solution)/shard_map/ppermute | solution.py:33
  109.5 0.0 copy-done.2
  109.5 0.8 fusion.54
  110.3 0.8 convolution_add_fusion.2
  111.1 19.3 %collective-permute-done.5 = bf16[2,256,1024]{1,2,0:T(8,128)(2,1)S(1)} collective-permute-done((bf16[2,256,1024]{1,2,0:T(8,128)(2,1)S(1)}, bf16[2,256,1024]{1,2,0:T(8,128)(2,1)S(1)}, u32[]{:S(2)}, u32[]{:S(2)}) %collective-permute-start.5) | collective-permute-done | bytes 1048608 | tf_op jit(solution)/shard_map/ppermute | solution.py:33
  130.4 0.8 fusion.42
  131.2 0.5 collective-permute-done.6
  131.7 0.8 fusion.41
  132.5 0.8 fusion.37
  133.3 1.6 fusion.38
  134.8 0.0 reduce-scatter.2.cloned.1.call-update
  134.8 6.3 %fusion.28 = bf16[8,128,512]{2,1,0:T(8,128)(2,1)S(1)} fusion(bf16[96,8,8,128]{3,2,1,0:T(8,128)(2,1)} %fusion.26, f32[8,512,768]{1,2,0:T(8,128)} %get-tuple-element.19, f32[8,512]{1,0:T(8,128)S(1)} %get-tuple-element.18), kind=kOutput, calls=%fused_computation.34 | convolution fusion | flops 812122112 | bytes 15220736 | tf_op jit(solution)/shard_map/htk,khd->thd/dot_general | solution.py:93
  141.1 1.3 copy.50
  142.5 18.3 %fusion.33 = bf16[8,128,512]{2,1,0:T(8,128)(2,1)S(1)} fusion(bf16[768,8,128]{0,2,1:T(8,128)(2,1)} %bitcast.136, f32[8,768,512]{2,1,0:T(8,128)} %fusion.21, f32[8,512,768]{1,2,0:T(8,128)} %get-tuple-element.19, f32[8,512]{1,0:T(8,128)S(1)} %get-tuple-element.18), kind=kOutput, calls=%fused_computation.35 | convolution fusion | flops 827855616 | bytes 27803648 | tf_op jit(solution)/shard_map/htk,khd->thd/dot_general | solution.py:103
  160.7 1.3 copy.51
  162.1 0.0 reduce-scatter.2.cloned.1.call-done
  (5 shorter events, 0.0 us)
Async XLA Ops:
  7.2 38.0 %copy-start = (bf16[1024,1024]{1,0:T(8,128)(2,1)S(1)}, bf16[1024,1024]{1,0:T(8,128)(2,1)}, u32[]{:S(2)}) copy-start(bf16[1024,1024]{1,0:T(8,128)(2,1)} %param.9) | copy-start | bytes 6291460
  7.2 24.1 %copy-start.5 = (bf16[512,1024]{1,0:T(8,128)(2,1)S(1)}, bf16[512,1024]{1,0:T(8,128)(2,1)}, u32[]{:S(2)}) copy-start(bf16[512,1024]{1,0:T(8,128)(2,1)} %param.6) | copy-start | bytes 3145732
  7.2 154.9 %reduce-scatter.2.cloned.1.call-start = ((), (), s32[]{:S(2)}) async-start(), calls=%async_computation.1 | async-start | bytes 655360 | tf_op jit(solution)/shard_map/reduce_scatter | solution.py:131
  7.2 8.3 %collective-permute-start = (bf16[256,256]{1,0:T(8,128)(2,1)}, bf16[256,256]{1,0:T(8,128)(2,1)S(1)}, u32[]{:S(2)}, u32[]{:S(2)}) collective-permute-start(bf16[256,256]{1,0:T(8,128)(2,1)} %param.7), channel_id=1, source_target_pairs={{0,4},{4,8},{8,12},{1,5},{5,9},{9,13},{2,6},{6,10},{10,14},{3,7},{... | collective-permute-start | bytes 393224 | tf_op jit(solution)/shard_map/ppermute | solution.py:22
  12.4 7.1 %collective-permute-start.1 = (bf16[256,256]{1,0:T(8,128)(2,1)}, bf16[256,256]{1,0:T(8,128)(2,1)S(1)}, u32[]{:S(2)}, u32[]{:S(2)}) collective-permute-start(bf16[256,256]{1,0:T(8,128)(2,1)} %param.7), channel_id=1, source_target_pairs={{4,0},{8,4},{12,8},{5,1},{9,5},{13,9},{6,2},{10,6},{14,10},{7,3},{... | collective-permute-start | bytes 393224 | tf_op jit(solution)/shard_map/ppermute | solution.py:25
  19.5 9.7 %collective-permute-start.2 = (bf16[768,256]{1,0:T(8,128)(2,1)S(1)}, bf16[768,256]{1,0:T(8,128)(2,1)}, u32[]{:S(2)}, u32[]{:S(2)}) collective-permute-start(bf16[768,256]{1,0:T(8,128)(2,1)S(1)} %constant_dynamic-update-slice_fusion), channel_id=1, source_target_pairs={{0,1},{1,2},{2,3},{3,0},{4,5},{5,6},{6,7},{7,4},{8,9},{9,10},{10,1... | collective-permute-start | bytes 1179656 | tf_op jit(solution)/shard_map/ppermute | solution.py:57
  19.6 14.5 %collective-permute-start.4 = (bf16[768,256]{1,0:T(8,128)(2,1)S(1)}, bf16[768,256]{1,0:T(8,128)(2,1)}, u32[]{:S(2)}, u32[]{:S(2)}) collective-permute-start(bf16[768,256]{1,0:T(8,128)(2,1)S(1)} %constant_dynamic-update-slice_fusion), channel_id=1, source_target_pairs={{1,0},{2,1},{3,2},{0,3},{5,4},{6,5},{7,6},{4,7},{9,8},{10,9},{11,1... | collective-permute-start | bytes 1179656 | tf_op jit(solution)/shard_map/ppermute | solution.py:59
  29.2 7.5 %collective-permute-start.3 = (bf16[768,256]{1,0:T(8,128)(2,1)}, bf16[768,256]{1,0:T(8,128)(2,1)}, u32[]{:S(2)}, u32[]{:S(2)}) collective-permute-start(bf16[768,256]{1,0:T(8,128)(2,1)} %collective-permute-done.2), channel_id=1, source_target_pairs={{0,1},{1,2},{2,3},{3,0},{4,5},{5,6},{6,7},{7,4},{8,9},{9,10},{10,1... | collective-permute-start | bytes 1179656 | tf_op jit(solution)/shard_map/ppermute | solution.py:57
  45.1 4.6 %copy-start.1 = (bf16[1024,1024]{1,0:T(8,128)(2,1)S(1)}, bf16[1024,1024]{1,0:T(8,128)(2,1)}, u32[]{:S(2)}) copy-start(bf16[1024,1024]{1,0:T(8,128)(2,1)} %param.8) | copy-start | bytes 6291460
  45.1 4.6 %copy-start.4 = (bf16[768,4,256]{0,2,1:T(8,128)(2,1)S(1)}, bf16[768,4,256]{0,2,1:T(8,128)(2,1)}, u32[]{:S(2)}) copy-start(bf16[768,4,256]{0,2,1:T(8,128)(2,1)} %copy.37) | copy-start | bytes 4718596
  55.3 7.7 %copy-start.6 = (pred[96,8,4,128]{3,1,2,0:T(8,128)(4,1)S(1)}, pred[96,8,4,128]{3,1,2,0:T(8,128)(4,1)}, u32[]{:S(2)}) copy-start(pred[96,8,4,128]{3,1,2,0:T(8,128)(4,1)} %copy.70) | copy-start | bytes 1179652
  100.9 1.9 %copy-start.3 = (bf16[768,8,128]{0,2,1:T(8,128)(2,1)S(1)}, bf16[768,8,128]{0,2,1:T(8,128)(2,1)}, u32[]{:S(2)}) copy-start(bf16[768,8,128]{0,2,1:T(8,128)(2,1)} %fusion.23) | copy-start | bytes 4718596
  103.0 6.5 %copy-start.2 = (bf16[1024,1024]{1,0:T(8,128)(2,1)S(1)}, bf16[1024,1024]{1,0:T(8,128)(2,1)}, u32[]{:S(2)}) copy-start(bf16[1024,1024]{1,0:T(8,128)(2,1)} %param.8) | copy-start | bytes 6291460
  103.1 27.3 %collective-permute-start.5 = (bf16[2,256,1024]{1,2,0:T(8,128)(2,1)S(1)}, bf16[2,256,1024]{1,2,0:T(8,128)(2,1)S(1)}, u32[]{:S(2)}, u32[]{:S(2)}) collective-permute-start(bf16[2,256,1024]{1,2,0:T(8,128)(2,1)S(1)} %pad_maximum_fusion.1), channel_id=1, source_target_pairs={{4,0},{8,4},{12,8},{5,1},{9,5},{13,9},{6,2},{10,6},{14,10},{7,3},{... | collective-permute-start | bytes 3145736 | tf_op jit(solution)/shard_map/ppermute | solution.py:33
  104.7 27.0 %collective-permute-start.6 = (bf16[2,256,1024]{1,2,0:T(8,128)(2,1)S(1)}, bf16[2,256,1024]{1,2,0:T(8,128)(2,1)S(1)}, u32[]{:S(2)}, u32[]{:S(2)}) collective-permute-start(bf16[2,256,1024]{1,2,0:T(8,128)(2,1)S(1)} %pad_maximum_fusion.2), channel_id=1, source_target_pairs={{0,4},{4,8},{8,12},{1,5},{5,9},{9,13},{2,6},{6,10},{10,14},{3,7},{... | collective-permute-start | bytes 3145736 | tf_op jit(solution)/shard_map/ppermute | solution.py:33
Sparse Core Ops, SparseCore 0:
  135.0 22.9 reduce-scatter.1
